TPU v7x, 256 devices: a whole 4x4x8 slice. The times are simulated.
256 devices in a mesh: mp: 8 (over z), dp: 32 (over y, x, core).
Axes of the slice: x: 4, y: 4, z: 8, core: 2. Of those that a mesh axis runs over, the one named last changes fastest.
Arguments:
- gate_partials: bfloat16 [32, 128, 73728], P('dp', 'mp'), as said below
- up_partials: bfloat16 [32, 128, 73728], P('dp', 'mp'), as said below
- gate_weight: float32 [128, 73728], P('mp', 'dp'), may hold values from -6 to 6
- up_weight: float32 [128, 73728], P('mp', 'dp'), may hold values from -6 to 6
- row_state: float32 [2, 128], P(None, 'mp'), may hold values from 0.1 to 10
- col_state: float32 [2, 73728], P(None, 'dp'), may hold values from 0.1 to 10
Outputs:
- new_gate: float32 [128, 73728], P('mp', 'dp')
- new_up: float32 [128, 73728], P('mp', 'dp')
- new_rows: float32 [2, 128], P(None, 'mp')
- new_cols: float32 [2, 73728], P(None, 'dp')
Inputs may be any that keep to these rules, and one draw needn't show every extreme that they name: `gate_partials`: partial gradients of one weight slab; entries are finite. `up_partials`: partial gradients of one weight slab; entries are finite.
All inputs are finite; a program needn't handle non-finite values.
Results may differ from a plain program's by a relative error of at most 0.0003.
Values sent between devices are 32-bit elements; how exact they have to be, the bound alone decides.
A program may use at most 64 MiB of HBM per device.

v0:
```python
import jax
import jax.numpy as jnp
from jax import lax
from jax.sharding import PartitionSpec as P

second_decay = 0.8
clip_limit = 1.0
step_size = 0.5


def on_device(gate_partials, up_partials, gate_weight, up_weight, row_state, col_state):
    gate_grad = lax.psum_scatter(
        gate_partials.astype(jnp.float32), "dp", scatter_dimension=2, tiled=True
    )
    up_grad = lax.psum_scatter(
        up_partials.astype(jnp.float32), "dp", scatter_dimension=2, tiled=True
    )
    gradient = jnp.concatenate([gate_grad, up_grad], axis=0)
    squares = gradient * gradient
    row_part = jnp.sum(squares, axis=2)
    col_part = jnp.sum(squares, axis=1)
    all_rows = row_state.shape[1] * lax.axis_size("mp")
    all_cols = col_state.shape[1] * lax.axis_size("dp")
    row_sums = lax.psum(row_part, "dp")
    col_sums = lax.psum(col_part, "mp")
    new_rows = second_decay * row_state + (1.0 - second_decay) * row_sums / all_cols
    new_cols = second_decay * col_state + (1.0 - second_decay) * col_sums / all_rows
    row_mean = lax.psum(jnp.sum(new_rows, axis=1), "mp") / all_rows
    second = new_rows[:, :, None] * new_cols[:, None, :] / row_mean[:, None, None]
    update = gradient / jnp.sqrt(second)
    update_sums = lax.psum(jnp.sum(update * update, axis=(1, 2)), ("mp", "dp"))
    rms_value = jnp.sqrt(update_sums / (all_rows * all_cols))
    factor = 1.0 / jnp.maximum(1.0, rms_value / clip_limit)
    new_gate = gate_weight - step_size * factor[0] * update[0]
    new_up = up_weight - step_size * factor[1] * update[1]
    return (new_gate, new_up, new_rows, new_cols)


def solution(mesh):
    placed = (
        P("dp", "mp", None),
        P("dp", "mp", None),
        P("mp", "dp"),
        P("mp", "dp"),
        P(None, "mp"),
        P(None, "dp"),
    )
    return jax.shard_map(
        on_device,
        mesh=mesh,
        in_specs=placed,
        out_specs=(P("mp", "dp"), P("mp", "dp"), P(None, "mp"), P(None, "dp")),
        check_vma=False,
    )
```

profile of v0, /device:TPU:1, one launch (start us, length us, event | category | flops | bytes accessed | tf_op | source)
XLA Modules:
  0.0 377.8 jit_solution(11567926942905543371)
XLA Ops:
  7.2 0.0 copy-start
  7.2 0.0 reduce-scatter.3.cloned.1.call-start
  7.2 4.2 %convert_element_type.6 = f32[1,16,73728]{2,1,0:T(8,128)} convert(bf16[1,16,73728]{2,1,0:T(8,128)(2,1)} %param.6) | non-fusion elementwise | flops 1179648 | bytes 7077888 | tf_op jit(solution)/shard_map/convert_element_type | solution.py:13
  11.5 0.0 reduce-scatter.3.cloned.1.call-update
  11.5 0.0 copy-start.6
  11.5 0.0 copy-start.4
  11.5 0.0 reduce-scatter.5.cloned.1.call-start
  11.6 0.0 copy-done
  11.6 2.5 convert_element_type.7
  14.1 0.0 reduce-scatter.5.cloned.1.call-update
  14.1 91.4 %reduce-scatter.3.cloned.1.call-done = f32[1,16,2304]{2,1,0:T(8,128)} async-done(((f32[1,16,73728]{2,1,0:T(8,128)}), f32[1,16,2304]{2,1,0:T(8,128)}) %reduce-scatter.3.cloned.1.call-update) | async-done | bytes 147472 | tf_op jit(solution)/shard_map/reduce_scatter | solution.py:12
  105.5 0.9 constant_dynamic-update-slice_fusion.1
  106.4 94.3 %reduce-scatter.5.cloned.1.call-done = f32[1,16,2304]{2,1,0:T(8,128)} async-done(((f32[1,16,73728]{2,1,0:T(8,128)}), f32[1,16,2304]{2,1,0:T(8,128)}) %reduce-scatter.5.cloned.1.call-update) | async-done | bytes 147472 | tf_op jit(solution)/shard_map/reduce_scatter | solution.py:15
  200.7 0.9 constant_dynamic-update-slice_fusion
  201.7 0.1 multiply_reduce_fusion.1
  201.8 64.3 %psum.28 = f32[2,16]{1,0:T(2,128)S(1)} all-reduce(f32[2,16]{1,0:T(2,128)S(1)} %get-tuple-element.5), channel_id=1, replica_groups=mesh['mp'=8,'dp'=32] {'dp'}, use_global_device_ids=true, to_apply=%region_3.0 | all-reduce | flops 32 | bytes 256 | tf_op jit(solution)/shard_map/psum | solution.py:24
  266.1 0.1 fusion.4
  266.2 23.1 %all-reduce = (f32[2]{0:T(128)S(1)}, f32[2,2304]{1,0:T(2,128)S(1)}) all-reduce(f32[2]{0:T(128)S(1)} %get-tuple-element.10, f32[2,2304]{1,0:T(2,128)S(1)} %get-tuple-element.4), channel_id=1, replica_groups=mesh['mp'=8,'dp'=32] {'mp'}, use_global_device_ids=true, to_apply=%region_7.0 | all-reduce | flops 4610 | bytes 36880 | tf_op jit(solution)/shard_map/psum | solution.py:28
  289.3 0.0 copy-done.4
  289.4 0.0 copy-start.3
  289.4 0.2 multiply_reduce_fusion
  289.6 78.6 %psum.31 = f32[2]{0:T(128)S(1)} all-reduce(f32[2]{0:T(128)S(1)} %get-tuple-element.8), channel_id=1, replica_groups=mesh['mp'=8,'dp'=32] {'mp','dp'}, use_global_device_ids=true, to_apply=%region_9.0 | all-reduce | flops 2 | bytes 16 | tf_op jit(solution)/shard_map/psum | solution.py:31
  368.3 0.6 fusion.5
  370.2 0.7 fusion.1
  (11 shorter events, 0.0 us)
Async XLA Ops:
  7.2 4.4 %copy-start = (bf16[1,16,73728]{2,1,0:T(8,128)(2,1)S(1)}, bf16[1,16,73728]{2,1,0:T(8,128)(2,1)}, u32[]{:S(2)}) copy-start(bf16[1,16,73728]{2,1,0:T(8,128)(2,1)} %param.7) | copy-start | bytes 7077892
  7.2 98.3 %reduce-scatter.3.cloned.1.call-start = ((), (), s32[]{:S(2)}) async-start(), calls=%async_computation.2 | async-start | bytes 4866048 | tf_op jit(solution)/shard_map/reduce_scatter | solution.py:12
  11.5 254.6 %copy-start.6 = (f32[2,16]{1,0:T(2,128)S(1)}, f32[2,16]{1,0:T(2,128)}, u32[]{:S(2)}) copy-start(f32[2,16]{1,0:T(2,128)} %param.10) | copy-start | bytes 388
  11.5 277.8 %copy-start.4 = (f32[2,2304]{1,0:T(2,128)S(1)}, f32[2,2304]{1,0:T(2,128)}, u32[]{:S(2)}) copy-start(f32[2,2304]{1,0:T(2,128)} %param.11) | copy-start | bytes 55300
  11.5 189.2 %reduce-scatter.5.cloned.1.call-start = ((), (), s32[]{:S(2)}) async-start(), calls=%async_computation.3 | async-start | bytes 4866048 | tf_op jit(solution)/shard_map/reduce_scatter | solution.py:15
  14.0 356.1 %copy-start.1 = (f32[16,2304]{1,0:T(8,128)S(1)}, f32[16,2304]{1,0:T(8,128)}, u32[]{:S(2)}) copy-start(f32[16,2304]{1,0:T(8,128)} %param.9) | copy-start | bytes 442372
  14.0 356.1 %copy-start.2 = (f32[16,2304]{1,0:T(8,128)S(1)}, f32[16,2304]{1,0:T(8,128)}, u32[]{:S(2)}) copy-start(f32[16,2304]{1,0:T(8,128)} %param.8) | copy-start | bytes 442372
  266.2 104.7 %copy-start.5 = (f32[2,16]{1,0:T(2,128)}, f32[2,16]{1,0:T(2,128)S(1)}, u32[]{:S(2)}) copy-start(f32[2,16]{1,0:T(2,128)S(1)} %get-tuple-element.11) | copy-start | bytes 388
  289.4 81.6 %copy-start.3 = (f32[2,2304]{1,0:T(2,128)}, f32[2,2304]{1,0:T(2,128)S(1)}, u32[]{:S(2)}) copy-start(f32[2,2304]{1,0:T(2,128)S(1)} %multiply_add_fusion) | copy-start | bytes 55300
Sparse Core Ops, SparseCore 0:
  12.0 93.4 reduce-scatter.2
  110.0 90.6 reduce-scatter.4
where the time goes:
time: 378 us
  waiting for transfers between devices  186 us (49%)
  blocking collectives  166 us (44%)
  between operations  15.4 us (4%)
  other arithmetic  7.95 us (2%)
    reduce_scatter x1, waiting for transfers between devices, on_device(): lax.psum_scatter(up_partials.astype(jnp.float32), 'dp', scatter_dimension...  94.3 us
    reduce_scatter x1, waiting for transfers between devices, on_device(): lax.psum_scatter(gate_partials.astype(jnp.float32), 'dp', scatter_dimensi...  91.4 us
    psum x1, blocking collectives, on_device(): update_sums = lax.psum(jnp.sum(update * update, axis=(1, 2)), ('mp', 'dp'))  78.6 us
    psum x1, blocking collectives, on_device(): row_sums = lax.psum(row_part, 'dp')  64.3 us
    psum x1, blocking collectives, on_device(): row_mean = lax.psum(jnp.sum(new_rows, axis=1), 'mp') / all_rows  23.1 us
  transfers between devices with their start and end apart: 2, of which 2 were waited for; matrix products, arithmetic and copies ran while one was open for 1% of the time, Pallas kernels for 0%

commit v1 on v0

v1 whole, which is shorter than its diff:
```python
import functools

import jax
import jax.numpy as jnp
from jax import lax
from jax.experimental import pallas as pl
from jax.experimental.pallas import tpu as pltpu
from jax.sharding import PartitionSpec as P

ROWS = 128
FF = 73728
DECAY = 0.8
STEP = 0.5
NZ, NY, NX, NC = 8, 4, 4, 2
NDP = NY * NX * NC
BLOCK = FF // NDP
HALF = 8
LANE = 128
WIDE = 3 * LANE
CHUNKS = tuple((m, j * 2 * WIDE, WIDE) for m in range(2) for j in range(BLOCK // (2 * WIDE)))
K = len(CHUNKS)
MESH = pl.DeviceIdType.MESH


def kernel(
    gate_hbm, up_hbm, gate_w_hbm, up_w_hbm, rows_hbm, cols_hbm,
    new_gate_hbm, new_up_hbm, new_rows_hbm, new_cols_hbm,
    inb, give, work, far, acc, direct, far2, acc2, direct2, grad,
    weight, row_state, col_state, new_rows, new_cols, col_all, row_all, sum_all, result,
    in_sem, core_send, core_recv, s1_send, s1_recv, s2_send, s2_recv,
    col_send, col_recv, row_send, row_recv, sum_send, sum_recv, w_sem, out_sem,
):
    z = lax.axis_index("mp")
    d = lax.axis_index("dp")
    y, x, c = d // (NX * NC), (d // NC) % NX, d % NC

    def device(zz, yy, xx, cc):
        return (lax.rem(zz, NZ), (lax.rem(yy, NY) * NX + lax.rem(xx, NX)) * NC + lax.rem(cc, NC))

    sibling = device(z, y, x, c + 1)
    step_x = (device(z, y, x + 1, c), device(z, y, x + NX - 1, c))
    step_y = (device(z, y + 1, x, c), device(z, y + NY - 1, x, c))
    plane = [
        device(z, y + dy, x + dx, c + dc)
        for dy in (2, 1, 3, 0) for dx in (2, 1, 3, 0) for dc in (1, 0) if (dy, dx, dc) != (0, 0, 0)
    ]
    column = [device(z + k, y, x, c) for k in (4, 3, 5, 2, 6, 1, 7)]

    barrier = pltpu.get_barrier_semaphore()
    for peer in column + plane:
        pl.semaphore_signal(barrier, 1, device_id=peer, device_id_type=MESH)

    partials = (gate_hbm, up_hbm)

    def load(k):
        m, first, wide = CHUNKS[k]

        def one(i, carry):
            ry, rx = i // NX, i % NX
            owner = (lax.rem(y + ry, NY) * NX + lax.rem(x + rx, NX)) * NC
            for side in range(2):
                core = (1 - c) if side == 0 else c
                start = pl.multiple_of((owner + core) * BLOCK + first, LANE)
                pltpu.make_async_copy(
                    partials[m].at[0, :, pl.ds(start, 2 * wide)], inb.at[k, side, ry, rx], in_sem.at[k, side]
                ).start()
            return carry

        lax.fori_loop(0, NY * NX, one, 0)

    for k in range(K):
        load(k)
    pltpu.make_async_copy(gate_w_hbm, weight.at[0], w_sem.at[0]).start()
    pltpu.make_async_copy(up_w_hbm, weight.at[1], w_sem.at[1]).start()
    pltpu.make_async_copy(rows_hbm, row_state, w_sem.at[2]).start()
    pltpu.make_async_copy(cols_hbm, col_state, w_sem.at[3]).start()

    def wait_load(k, side):
        pltpu.make_async_copy(inb.at[k, side], inb.at[k, side], in_sem.at[k, side]).wait()

    started = []

    def send(src, dst, send_sem, recv_sem, target):
        copy = pltpu.make_async_remote_copy(
            src_ref=src, dst_ref=dst, send_sem=send_sem, recv_sem=recv_sem, device_id=target, device_id_type=MESH
        )
        copy.start()
        started.append(copy)
        return copy

    def convert(k):
        wait_load(k, 0)
        wide = CHUNKS[k][2]

        def one(i, carry):
            ry, rx = i // NX, i % NX
            value = inb[k, 0, ry, rx].astype(jnp.float32)
            for h in range(2):
                part = value[:, h * wide : (h + 1) * wide]
                give[k, 0, h, rx, ry] = part[:HALF]
                give[k, 1, h, ry, rx] = part[HALF:]
            return carry

        lax.fori_loop(0, NY * NX, one, 0)

    def exchange(k):
        return send(give.at[k], work.at[k], core_send.at[k], core_recv.at[k], sibling)

    def add_own(k):
        wait_load(k, 1)
        wide = CHUNKS[k][2]

        def one(i, carry):
            ry, rx = i // NX, i % NX
            value = inb[k, 1, ry, rx].astype(jnp.float32)
            for h in range(2):
                part = value[:, h * wide : (h + 1) * wide]
                work[k, 0, h, rx, ry] = work[k, 0, h, rx, ry] + part[:HALF]
                work[k, 1, h, ry, rx] = work[k, 1, h, ry, rx] + part[HALF:]
            return carry

        lax.fori_loop(0, NY * NX, one, 0)

    near = (1, 3)
    pairs = [(p, h) for h in range(2) for p in range(2)]
    copies = {}

    def first_sends(k):
        for p, h in pairs:
            step = (step_x, step_y)[p]
            copies[k, p, h, "far"] = send(
                work.at[k, p, h, 2], far.at[k, p, h], s1_send.at[k, p, h, 0], s1_recv.at[k, p, h, 0], step[h])
        for p, h in pairs:
            step = (step_x, step_y)[p]
            copies[k, p, h, "direct"] = send(
                work.at[k, p, h, near[1 - h]], direct.at[k, p, h], s1_send.at[k, p, h, 1], s1_recv.at[k, p, h, 1],
                step[1 - h])

    def first_join(k):
        for p, h in pairs:
            step = (step_x, step_y)[p]
            copies[k, p, h, "far"].wait_recv()
            work[k, p, h, near[h]] = work[k, p, h, near[h]] + far[k, p, h]
            copies[k, p, h, "acc"] = send(
                work.at[k, p, h, near[h]], acc.at[k, p, h], s1_send.at[k, p, h, 2], s1_recv.at[k, p, h, 2], step[h])

    def second_sends(k):
        for p, h in pairs:
            step = (step_y, step_x)[p]
            copies[k, p, h, "direct"].wait_recv()
            copies[k, p, h, "acc"].wait_recv()
            work[k, p, h, 0] = work[k, p, h, 0] + direct[k, p, h] + acc[k, p, h]
            copies[k, p, h, "far2"] = send(
                work.at[k, p, h, 0, 2], far2.at[k, p, h], s2_send.at[k, p, h, 0], s2_recv.at[k, p, h, 0], step[h])
            copies[k, p, h, "direct2"] = send(
                work.at[k, p, h, 0, near[1 - h]], direct2.at[k, p, h], s2_send.at[k, p, h, 1],
                s2_recv.at[k, p, h, 1], step[1 - h])

    def second_join(k):
        for p, h in pairs:
            step = (step_y, step_x)[p]
            copies[k, p, h, "far2"].wait_recv()
            work[k, p, h, 0, near[h]] = work[k, p, h, 0, near[h]] + far2[k, p, h]
            copies[k, p, h, "acc2"] = send(
                work.at[k, p, h, 0, near[h]], acc2.at[k, p, h], s2_send.at[k, p, h, 2], s2_recv.at[k, p, h, 2],
                step[h])

    lane_sums = [None, None]

    def lanes(value):
        total = value[:, :LANE]
        for j in range(1, value.shape[1] // LANE):
            total = total + value[:, j * LANE : (j + 1) * LANE]
        return total

    def finish(k):
        m, first, wide = CHUNKS[k]
        for p, h in pairs:
            copies[k, p, h, "direct2"].wait_recv()
            copies[k, p, h, "acc2"].wait_recv()
            grad[m, p * HALF : (p + 1) * HALF, first + h * wide : first + (h + 1) * wide] = (
                work[k, p, h, 0, 0] + direct2[k, p, h] + acc2[k, p, h])
        g = grad[m, :, first : first + 2 * wide]
        squares = g * g
        col_all[k, z] = jnp.sum(squares, axis=0, keepdims=True)
        for i, peer in enumerate(column):
            send(col_all.at[k, z], col_all.at[k, z], col_send.at[k, i], col_recv.at[k, i], peer)
        part = lanes(squares)
        lane_sums[m] = part if lane_sums[m] is None else lane_sums[m] + part

    def wait_columns(k):
        for i in range(NZ - 1):
            source = lax.rem(z + NZ - (4, 3, 5, 2, 6, 1, 7)[i], NZ)
            pltpu.make_async_remote_copy(
                src_ref=col_all.at[k, source], dst_ref=col_all.at[k, source], send_sem=col_send.at[k, i],
                recv_sem=col_recv.at[k, i], device_id=sibling, device_id_type=MESH).wait_recv()

    for k in range(K):
        convert(k)
        if k == 0:
            pl.semaphore_wait(barrier, len(plane) + len(column))
        copies[k, "core"] = exchange(k)
        if k > 0:
            copies[k - 1, "core"].wait_recv()
            add_own(k - 1)
            first_sends(k - 1)
    copies[K - 1, "core"].wait_recv()
    add_own(K - 1)
    first_sends(K - 1)
    for k in range(K):
        first_join(k)
    for k in range(K):
        second_sends(k)
    for k in range(K):
        second_join(k)
    for k in range(K):
        finish(k)

    row_id = lax.broadcasted_iota(jnp.int32, (16, LANE), 0)
    lane_id = lax.broadcasted_iota(jnp.int32, (16, LANE), 1)
    lane_one = lax.broadcasted_iota(jnp.int32, (1, LANE), 1)
    small_row = lax.broadcasted_iota(jnp.int32, (16, 16), 0)
    small_lane = lax.broadcasted_iota(jnp.int32, (16, 16), 1)

    row_sums = [jnp.sum(lane_sums[m], axis=1, keepdims=True) for m in range(2)]
    for i in range(4):
        ref = (weight.at[0], weight.at[1], row_state, col_state)[i]
        pltpu.make_async_copy(ref, ref, w_sem.at[i]).wait()
    old_rows = [
        jnp.sum(jnp.where(small_row == small_lane, row_state[m : m + 1, :], 0.0), axis=1, keepdims=True)
        for m in range(2)
    ]

    scaled = [None, None]
    for k in range(K):
        m, first, wide = CHUNKS[k]
        wait_columns(k)
        total = col_all[k, 0]
        for j in range(1, NZ):
            total = total + col_all[k, j]
        span = slice(first, first + 2 * wide)
        fresh = DECAY * col_state[m : m + 1, span] + (1.0 - DECAY) * total / ROWS
        new_cols[m : m + 1, span] = fresh
        g = grad[m, :, span]
        part = lanes(g * g * (1.0 / fresh))
        scaled[m] = part if scaled[m] is None else scaled[m] + part
    scaled = [jnp.sum(scaled[m], axis=1, keepdims=True) for m in range(2)]

    packed = jnp.zeros((16, LANE), jnp.float32)
    for q, value in enumerate(row_sums + scaled):
        packed = jnp.where(lane_id == row_id + 16 * q, value, packed)
    row_all[d] = jnp.sum(packed, axis=0, keepdims=True)
    for i, peer in enumerate(plane):
        send(row_all.at[d], row_all.at[d], row_send.at[i], row_recv.at[i], peer)

    out_cols = pltpu.make_async_copy(new_cols, new_cols_hbm, out_sem.at[0])
    out_cols.start()
    for m in range(2):
        grad[m] = grad[m] * lax.rsqrt(new_cols[m : m + 1, :])

    offsets = [
        (dy, dx, dc) for dy in (2, 1, 3, 0) for dx in (2, 1, 3, 0) for dc in (1, 0) if (dy, dx, dc) != (0, 0, 0)
    ]
    for i, (dy, dx, dc) in enumerate(offsets):
        source = device(z, y + NY - dy, x + NX - dx, c + dc)[1]
        pltpu.make_async_remote_copy(
            src_ref=row_all.at[source], dst_ref=row_all.at[source], send_sem=row_send.at[i],
            recv_sem=row_recv.at[i], device_id=sibling, device_id_type=MESH).wait_recv()
    total = row_all[0]
    for j in range(1, NDP):
        total = total + row_all[j]
    spread = jnp.broadcast_to(total, (16, LANE))
    part = [
        jnp.sum(jnp.where(lane_id == row_id + 16 * q, spread, 0.0), axis=1, keepdims=True) for q in range(4)
    ]
    fresh_rows = [DECAY * old_rows[m] + (1.0 - DECAY) * part[m] / FF for m in range(2)]
    message = jnp.zeros((1, LANE), jnp.float32)
    for m in range(2):
        message = jnp.where(lane_one == m, jnp.sum(part[2 + m] / fresh_rows[m], axis=0, keepdims=True), message)
        message = jnp.where(lane_one == 2 + m, jnp.sum(fresh_rows[m], axis=0, keepdims=True), message)
    sum_all[z] = message
    for i, peer in enumerate(column):
        send(sum_all.at[z], sum_all.at[z], sum_send.at[i], sum_recv.at[i], peer)

    for m in range(2):
        new_rows[m : m + 1, :] = jnp.sum(
            jnp.where(small_row == small_lane, fresh_rows[m], 0.0), axis=0, keepdims=True)
        grad[m] = grad[m] * lax.rsqrt(fresh_rows[m])
    out_rows = pltpu.make_async_copy(new_rows, new_rows_hbm, out_sem.at[1])
    out_rows.start()

    for i in range(NZ - 1):
        source = lax.rem(z + NZ - (4, 3, 5, 2, 6, 1, 7)[i], NZ)
        pltpu.make_async_remote_copy(
            src_ref=sum_all.at[source], dst_ref=sum_all.at[source], send_sem=sum_send.at[i],
            recv_sem=sum_recv.at[i], device_id=sibling, device_id_type=MESH).wait_recv()
    total = sum_all[0]
    for j in range(1, NZ):
        total = total + sum_all[j]
    outs = []
    for m in range(2):
        squares = jnp.sum(jnp.where(lane_one == m, total, 0.0), axis=1, keepdims=True)
        mean = jnp.sum(jnp.where(lane_one == 2 + m, total, 0.0), axis=1, keepdims=True) / ROWS
        root = jnp.sqrt(mean)
        rms = root * jnp.sqrt(squares / (ROWS * FF))
        scale = STEP * root / jnp.maximum(1.0, rms)
        result[m] = weight[m] - grad[m] * scale
        out = pltpu.make_async_copy(result.at[m], (new_gate_hbm, new_up_hbm)[m], out_sem.at[2 + m])
        out.start()
        outs.append(out)
    for copy in started:
        copy.wait_send()
    out_cols.wait()
    out_rows.wait()
    for out in outs:
        out.wait()


def on_device(gate_partials, up_partials, gate_weight, up_weight, row_state, col_state):
    f32 = jnp.float32
    dma = pltpu.SemaphoreType.DMA
    return pl.pallas_call(
        kernel,
        out_shape=(
            jax.ShapeDtypeStruct((16, BLOCK), f32),
            jax.ShapeDtypeStruct((16, BLOCK), f32),
            jax.ShapeDtypeStruct((2, 16), f32),
            jax.ShapeDtypeStruct((2, BLOCK), f32),
        ),
        in_specs=[pl.BlockSpec(memory_space=pl.ANY)] * 6,
        out_specs=(pl.BlockSpec(memory_space=pl.ANY),) * 4,
        scratch_shapes=[
            pltpu.VMEM((K, 2, NY, NX, 16, 2 * WIDE), jnp.bfloat16),
            pltpu.VMEM((K, 2, 2, 4, 4, HALF, WIDE), f32),
            pltpu.VMEM((K, 2, 2, 4, 4, HALF, WIDE), f32),
            pltpu.VMEM((K, 2, 2, 4, HALF, WIDE), f32),
            pltpu.VMEM((K, 2, 2, 4, HALF, WIDE), f32),
            pltpu.VMEM((K, 2, 2, 4, HALF, WIDE), f32),
            pltpu.VMEM((K, 2, 2, HALF, WIDE), f32),
            pltpu.VMEM((K, 2, 2, HALF, WIDE), f32),
            pltpu.VMEM((K, 2, 2, HALF, WIDE), f32),
            pltpu.VMEM((2, 16, BLOCK), f32),
            pltpu.VMEM((2, 16, BLOCK), f32),
            pltpu.VMEM((2, 16), f32),
            pltpu.VMEM((2, BLOCK), f32),
            pltpu.VMEM((2, 16), f32),
            pltpu.VMEM((2, BLOCK), f32),
            pltpu.VMEM((K, NZ, 1, 2 * WIDE), f32),
            pltpu.VMEM((NDP, 1, LANE), f32),
            pltpu.VMEM((NZ, 1, LANE), f32),
            pltpu.VMEM((2, 16, BLOCK), f32),
            dma((K, 2)),
            dma((K,)),
            dma((K,)),
            dma((K, 2, 2, 3)),
            dma((K, 2, 2, 3)),
            dma((K, 2, 2, 3)),
            dma((K, 2, 2, 3)),
            dma((K, NZ - 1)),
            dma((K, NZ - 1)),
            dma((NDP - 1,)),
            dma((NDP - 1,)),
            dma((NZ - 1,)),
            dma((NZ - 1,)),
            dma((4,)),
            dma((4,)),
        ],
        compiler_params=pltpu.CompilerParams(
            collective_id=0, has_side_effects=True, vmem_limit_bytes=48 * 1024 * 1024
        ),
    )(gate_partials, up_partials, gate_weight, up_weight, row_state, col_state)


def solution(mesh):
    placed = (
        P("dp", "mp", None),
        P("dp", "mp", None),
        P("mp", "dp"),
        P("mp", "dp"),
        P(None, "mp"),
        P(None, "dp"),
    )
    return jax.shard_map(
        on_device,
        mesh=mesh,
        in_specs=placed,
        out_specs=(P("mp", "dp"), P("mp", "dp"), P(None, "mp"), P(None, "dp")),
        check_vma=False,
    )
```

time: 378 us -> 72 us (0.19)
  waiting for transfers between devices: 186 us -> 0 us
  blocking collectives: 166 us -> 0 us
  Pallas kernels: 0 us -> 62 us
  between operations: 15.4 us -> 0.66 us
  other arithmetic: 7.95 us -> 0 us
  local copies, waits for them, and re-layouts: 2.47 us -> 9.03 us
    reduce_scatter x2 -> x0, waiting for transfers between devices: 186 us -> none  [the longest x1 94.3 us: on_device(): lax.psum_scatter(up_partials.astype(jnp.float32), 'dp', scatter_dimension...]
    psum x3 -> x0, blocking collectives: 166 us -> none  [the longest x1 78.6 us: on_device(): update_sums = lax.psum(jnp.sum(update * update, axis=(1, 2)), ('mp', 'dp'))]
    pallas_call x0 -> x1, Pallas kernels: none -> 62 us  [on_device(): pl.pallas_call(kernel, out_shape=(jax.ShapeDtypeStruct((16, BLOCK), f32),...]
    unnamed x15 -> x16, local copies, waits for them, and re-layouts: 0.95 us -> 9.03 us
    convert_element_type x2 -> x0, other arithmetic: 6.72 us -> none  [the longest x1 4.24 us: on_device(): gate_partials.astype(jnp.float32)]
  transfers between devices with their start and end apart: 2 -> 0, of which waited for: 2 -> 0; matrix products, arithmetic and copies ran while one was open for 1% -> 0% of each run, Pallas kernels for 0% -> 0%
where the time goes in v1:
time: 72 us; the launch traced here: 71.7 us
  Pallas kernels  62 us (86%)
  local copies, waits for them, and re-layouts  9.03 us (13%)
    pallas_call x1, Pallas kernels, on_device(): pl.pallas_call(kernel, out_shape=(jax.ShapeDtypeStruct((16, BLOCK), f32),...  62 us
    unnamed x16, local copies, waits for them, and re-layouts  9.03 us

profile of v1, /device:TPU:1, one launch (start us, length us, event | category | flops | bytes accessed | tf_op | source)
XLA Modules:
  0.0 71.7 jit_solution(9009310243052112324)
XLA Ops:
  0.6 0.0 copy-start
  0.6 1.7 %copy-done = bf16[1,16,73728]{2,1,0:T(8,128)(2,1)S(1)} copy-done((bf16[1,16,73728]{2,1,0:T(8,128)(2,1)S(1)}, bf16[1,16,73728]{2,1,0:T(8,128)(2,1)}, u32[]{:S(2)}) %copy-start) | copy-done | bytes 2359320
  2.3 0.0 copy-start.1
  2.3 1.7 %copy-done.1 = bf16[1,16,73728]{2,1,0:T(8,128)(2,1)S(1)} copy-done((bf16[1,16,73728]{2,1,0:T(8,128)(2,1)S(1)}, bf16[1,16,73728]{2,1,0:T(8,128)(2,1)}, u32[]{:S(2)}) %copy-start.1) | copy-done | bytes 2359320
  4.0 0.0 copy-start.2
  4.0 0.9 %copy-done.2 = f32[16,2304]{1,0:T(8,128)S(1)} copy-done((f32[16,2304]{1,0:T(8,128)S(1)}, f32[16,2304]{1,0:T(8,128)}, u32[]{:S(2)}) %copy-start.2) | copy-done | bytes 147480
  4.9 0.0 copy-start.3
  4.9 0.9 %copy-done.3 = f32[16,2304]{1,0:T(8,128)S(1)} copy-done((f32[16,2304]{1,0:T(8,128)S(1)}, f32[16,2304]{1,0:T(8,128)}, u32[]{:S(2)}) %copy-start.3) | copy-done | bytes 147480
  5.8 0.0 copy-start.4
  5.8 0.7 %copy-done.4 = f32[2,2304]{1,0:T(2,128)S(1)} copy-done((f32[2,2304]{1,0:T(2,128)S(1)}, f32[2,2304]{1,0:T(2,128)}, u32[]{:S(2)}) %copy-start.4) | copy-done | bytes 18456
  6.5 0.0 copy-start.5
  6.5 0.7 copy-done.5
  7.2 62.0 %shard_map.93 = (f32[16,2304]{1,0:T(8,128)S(1)}, f32[16,2304]{1,0:T(8,128)S(1)}, f32[2,16]{1,0:T(2,128)S(1)}, f32[2,2304]{1,0:T(2,128)S(1)}) custom-call(bf16[1,16,73728]{2,1,0:T(8,128)(2,1)S(1)} %copy-done, bf16[1,16,73728]{2,1,0:T(8,128)(2,1)S(1)} %copy-done.1, f32[16,2304]{1,0:T(8,128)S(1)} %copy-done.2, f32[16,2304]{1,0:T(8,128)S(1)} %copy-done.3, ...), custom_call_target="tpu_custom_call" | custom-call | tf_op jit(solution)/shard_map/pallas_call | solution.py:322
  69.2 0.7 copy.14
  69.9 0.7 copy.15
  70.6 0.6 copy.16
  71.1 0.6 copy.17
Async XLA Ops:
  0.6 1.7 %copy-start = (bf16[1,16,73728]{2,1,0:T(8,128)(2,1)S(1)}, bf16[1,16,73728]{2,1,0:T(8,128)(2,1)}, u32[]{:S(2)}) copy-start(bf16[1,16,73728]{2,1,0:T(8,128)(2,1)} %gate_hbm.1) | copy-start | bytes 7077892
  2.3 1.7 %copy-start.1 = (bf16[1,16,73728]{2,1,0:T(8,128)(2,1)S(1)}, bf16[1,16,73728]{2,1,0:T(8,128)(2,1)}, u32[]{:S(2)}) copy-start(bf16[1,16,73728]{2,1,0:T(8,128)(2,1)} %up_hbm.1) | copy-start | bytes 7077892
  4.0 0.9 %copy-start.2 = (f32[16,2304]{1,0:T(8,128)S(1)}, f32[16,2304]{1,0:T(8,128)}, u32[]{:S(2)}) copy-start(f32[16,2304]{1,0:T(8,128)} %gate_w_hbm.1) | copy-start | bytes 442372
  4.9 0.9 %copy-start.3 = (f32[16,2304]{1,0:T(8,128)S(1)}, f32[16,2304]{1,0:T(8,128)}, u32[]{:S(2)}) copy-start(f32[16,2304]{1,0:T(8,128)} %up_w_hbm.1) | copy-start | bytes 442372
  5.8 0.7 %copy-start.4 = (f32[2,2304]{1,0:T(2,128)S(1)}, f32[2,2304]{1,0:T(2,128)}, u32[]{:S(2)}) copy-start(f32[2,2304]{1,0:T(2,128)} %cols_hbm.1) | copy-start | bytes 55300
  6.5 0.7 copy-start.5

commit v2 on v1

--- a/solution.py
+++ b/solution.py
@@ -23,10 +23,10 @@
 
 
 def kernel(
-    gate_hbm, up_hbm, gate_w_hbm, up_w_hbm, rows_hbm, cols_hbm,
-    new_gate_hbm, new_up_hbm, new_rows_hbm, new_cols_hbm,
+    gate_hbm, up_hbm, rows_hbm, cols_hbm,
+    shape_hbm, sums_hbm, new_rows_hbm, new_cols_hbm,
     inb, give, work, far, acc, direct, far2, acc2, direct2, grad,
-    weight, row_state, col_state, new_rows, new_cols, col_all, row_all, sum_all, result,
+    row_state, col_state, new_rows, new_cols, col_all, row_all, sum_all, sums,
     in_sem, core_send, core_recv, s1_send, s1_recv, s2_send, s2_recv,
     col_send, col_recv, row_send, row_recv, sum_send, sum_recv, w_sem, out_sem,
 ):
@@ -46,37 +46,23 @@
     ]
     column = [device(z + k, y, x, c) for k in (4, 3, 5, 2, 6, 1, 7)]
 
+    partials = (gate_hbm, up_hbm)
+
+    loads = [pltpu.make_async_copy(partials[m].at[0], inb.at[m], in_sem.at[m]) for m in range(2)]
+    for copy in loads:
+        copy.start()
     barrier = pltpu.get_barrier_semaphore()
-    for peer in column + plane:
+    greeted = [*step_x, *step_y, sibling, *column]
+    for peer in greeted:
         pl.semaphore_signal(barrier, 1, device_id=peer, device_id_type=MESH)
-
-    partials = (gate_hbm, up_hbm)
-
-    def load(k):
+    pltpu.make_async_copy(rows_hbm, row_state, w_sem.at[0]).start()
+    pltpu.make_async_copy(cols_hbm, col_state, w_sem.at[1]).start()
+
+    def own_block(k, i, core):
         m, first, wide = CHUNKS[k]
-
-        def one(i, carry):
-            ry, rx = i // NX, i % NX
-            owner = (lax.rem(y + ry, NY) * NX + lax.rem(x + rx, NX)) * NC
-            for side in range(2):
-                core = (1 - c) if side == 0 else c
-                start = pl.multiple_of((owner + core) * BLOCK + first, LANE)
-                pltpu.make_async_copy(
-                    partials[m].at[0, :, pl.ds(start, 2 * wide)], inb.at[k, side, ry, rx], in_sem.at[k, side]
-                ).start()
-            return carry
-
-        lax.fori_loop(0, NY * NX, one, 0)
-
-    for k in range(K):
-        load(k)
-    pltpu.make_async_copy(gate_w_hbm, weight.at[0], w_sem.at[0]).start()
-    pltpu.make_async_copy(up_w_hbm, weight.at[1], w_sem.at[1]).start()
-    pltpu.make_async_copy(rows_hbm, row_state, w_sem.at[2]).start()
-    pltpu.make_async_copy(cols_hbm, col_state, w_sem.at[3]).start()
-
-    def wait_load(k, side):
-        pltpu.make_async_copy(inb.at[k, side], inb.at[k, side], in_sem.at[k, side]).wait()
+        owner = (lax.rem(y + i // NX, NY) * NX + lax.rem(x + i % NX, NX)) * NC + core
+        start = pl.multiple_of(owner * BLOCK + first, LANE)
+        return inb[m, :, pl.ds(start, 2 * wide)].astype(jnp.float32)
 
     started = []
 
@@ -89,37 +75,35 @@
         return copy
 
     def convert(k):
-        wait_load(k, 0)
         wide = CHUNKS[k][2]
 
         def one(i, carry):
             ry, rx = i // NX, i % NX
-            value = inb[k, 0, ry, rx].astype(jnp.float32)
+            value = own_block(k, i, 1 - c)
             for h in range(2):
                 part = value[:, h * wide : (h + 1) * wide]
                 give[k, 0, h, rx, ry] = part[:HALF]
                 give[k, 1, h, ry, rx] = part[HALF:]
             return carry
 
-        lax.fori_loop(0, NY * NX, one, 0)
+        lax.fori_loop(0, NY * NX, one, 0, unroll=4)
 
     def exchange(k):
         return send(give.at[k], work.at[k], core_send.at[k], core_recv.at[k], sibling)
 
     def add_own(k):
-        wait_load(k, 1)
         wide = CHUNKS[k][2]
 
         def one(i, carry):
             ry, rx = i // NX, i % NX
-            value = inb[k, 1, ry, rx].astype(jnp.float32)
+            value = own_block(k, i, c)
             for h in range(2):
                 part = value[:, h * wide : (h + 1) * wide]
                 work[k, 0, h, rx, ry] = work[k, 0, h, rx, ry] + part[:HALF]
                 work[k, 1, h, ry, rx] = work[k, 1, h, ry, rx] + part[HALF:]
             return carry
 
-        lax.fori_loop(0, NY * NX, one, 0)
+        lax.fori_loop(0, NY * NX, one, 0, unroll=4)
 
     near = (1, 3)
     pairs = [(p, h) for h in range(2) for p in range(2)]
@@ -196,9 +180,11 @@
                 recv_sem=col_recv.at[k, i], device_id=sibling, device_id_type=MESH).wait_recv()
 
     for k in range(K):
+        if k == 0 or CHUNKS[k][0] != CHUNKS[k - 1][0]:
+            loads[CHUNKS[k][0]].wait()
         convert(k)
         if k == 0:
-            pl.semaphore_wait(barrier, len(plane) + len(column))
+            pl.semaphore_wait(barrier, len(greeted))
         copies[k, "core"] = exchange(k)
         if k > 0:
             copies[k - 1, "core"].wait_recv()
@@ -223,8 +209,7 @@
     small_lane = lax.broadcasted_iota(jnp.int32, (16, 16), 1)
 
     row_sums = [jnp.sum(lane_sums[m], axis=1, keepdims=True) for m in range(2)]
-    for i in range(4):
-        ref = (weight.at[0], weight.at[1], row_state, col_state)[i]
+    for i, ref in enumerate((row_state, col_state)):
         pltpu.make_async_copy(ref, ref, w_sem.at[i]).wait()
     old_rows = [
         jnp.sum(jnp.where(small_row == small_lane, row_state[m : m + 1, :], 0.0), axis=1, keepdims=True)
@@ -288,6 +273,10 @@
         grad[m] = grad[m] * lax.rsqrt(fresh_rows[m])
     out_rows = pltpu.make_async_copy(new_rows, new_rows_hbm, out_sem.at[1])
     out_rows.start()
+    out_shape = pltpu.make_async_copy(grad, shape_hbm, out_sem.at[2])
+    out_shape.start()
+    for copy in started[:-len(column)]:
+        copy.wait_send()
 
     for i in range(NZ - 1):
         source = lax.rem(z + NZ - (4, 3, 5, 2, 6, 1, 7)[i], NZ)
@@ -297,21 +286,49 @@
     total = sum_all[0]
     for j in range(1, NZ):
         total = total + sum_all[j]
-    outs = []
+    sums[...] = total
+    out_sums = pltpu.make_async_copy(sums, sums_hbm, out_sem.at[3])
+    out_sums.start()
+    for copy in started[-len(column):]:
+        copy.wait_send()
+    for out in (out_cols, out_rows, out_shape, out_sums):
+        out.wait()
+
+
+def apply(
+    shape_hbm, sums_hbm, rows_hbm, cols_hbm, gate_w_hbm, up_w_hbm,
+    new_gate_hbm, new_up_hbm, new_rows_hbm, new_cols_hbm,
+    shape, sums, weight, in_sem, out_sem,
+):
+    loads = [
+        pltpu.make_async_copy(src, dst, in_sem.at[i])
+        for i, (src, dst) in enumerate((
+            (sums_hbm, sums), (shape_hbm.at[0], shape.at[0]), (gate_w_hbm, weight.at[0]),
+            (shape_hbm.at[1], shape.at[1]), (up_w_hbm, weight.at[1])))
+    ]
+    outs = [
+        pltpu.make_async_copy(rows_hbm, new_rows_hbm, out_sem.at[2]),
+        pltpu.make_async_copy(cols_hbm, new_cols_hbm, out_sem.at[3]),
+    ]
+    for copy in loads + outs:
+        copy.start()
+    loads[0].wait()
+    lane = lax.broadcasted_iota(jnp.int32, (1, LANE), 1)
+    total = sums[...]
+    scales = []
     for m in range(2):
-        squares = jnp.sum(jnp.where(lane_one == m, total, 0.0), axis=1, keepdims=True)
-        mean = jnp.sum(jnp.where(lane_one == 2 + m, total, 0.0), axis=1, keepdims=True) / ROWS
+        squares = jnp.sum(jnp.where(lane == m, total, 0.0), axis=1, keepdims=True)
+        mean = jnp.sum(jnp.where(lane == 2 + m, total, 0.0), axis=1, keepdims=True) / ROWS
         root = jnp.sqrt(mean)
         rms = root * jnp.sqrt(squares / (ROWS * FF))
-        scale = STEP * root / jnp.maximum(1.0, rms)
-        result[m] = weight[m] - grad[m] * scale
-        out = pltpu.make_async_copy(result.at[m], (new_gate_hbm, new_up_hbm)[m], out_sem.at[2 + m])
+        scales.append(STEP * root / jnp.maximum(1.0, rms))
+    for m in range(2):
+        loads[1 + 2 * m].wait()
+        loads[2 + 2 * m].wait()
+        weight[m] = weight[m] - shape[m] * scales[m]
+        out = pltpu.make_async_copy(weight.at[m], (new_gate_hbm, new_up_hbm)[m], out_sem.at[m])
         out.start()
         outs.append(out)
-    for copy in started:
-        copy.wait_send()
-    out_cols.wait()
-    out_rows.wait()
     for out in outs:
         out.wait()
 
@@ -319,18 +336,18 @@
 def on_device(gate_partials, up_partials, gate_weight, up_weight, row_state, col_state):
     f32 = jnp.float32
     dma = pltpu.SemaphoreType.DMA
-    return pl.pallas_call(
+    shape, sums, new_rows, new_cols = pl.pallas_call(
         kernel,
         out_shape=(
-            jax.ShapeDtypeStruct((16, BLOCK), f32),
-            jax.ShapeDtypeStruct((16, BLOCK), f32),
+            jax.ShapeDtypeStruct((2, 16, BLOCK), f32),
+            jax.ShapeDtypeStruct((1, LANE), f32),
             jax.ShapeDtypeStruct((2, 16), f32),
             jax.ShapeDtypeStruct((2, BLOCK), f32),
         ),
-        in_specs=[pl.BlockSpec(memory_space=pl.ANY)] * 6,
+        in_specs=[pl.BlockSpec(memory_space=pl.ANY)] * 4,
         out_specs=(pl.BlockSpec(memory_space=pl.ANY),) * 4,
         scratch_shapes=[
-            pltpu.VMEM((K, 2, NY, NX, 16, 2 * WIDE), jnp.bfloat16),
+            pltpu.VMEM((2, 16, FF), jnp.bfloat16),
             pltpu.VMEM((K, 2, 2, 4, 4, HALF, WIDE), f32),
             pltpu.VMEM((K, 2, 2, 4, 4, HALF, WIDE), f32),
             pltpu.VMEM((K, 2, 2, 4, HALF, WIDE), f32),
@@ -340,7 +357,6 @@
             pltpu.VMEM((K, 2, 2, HALF, WIDE), f32),
             pltpu.VMEM((K, 2, 2, HALF, WIDE), f32),
             pltpu.VMEM((2, 16, BLOCK), f32),
-            pltpu.VMEM((2, 16, BLOCK), f32),
             pltpu.VMEM((2, 16), f32),
             pltpu.VMEM((2, BLOCK), f32),
             pltpu.VMEM((2, 16), f32),
@@ -348,8 +364,8 @@
             pltpu.VMEM((K, NZ, 1, 2 * WIDE), f32),
             pltpu.VMEM((NDP, 1, LANE), f32),
             pltpu.VMEM((NZ, 1, LANE), f32),
-            pltpu.VMEM((2, 16, BLOCK), f32),
-            dma((K, 2)),
+            pltpu.VMEM((1, LANE), f32),
+            dma((2,)),
             dma((K,)),
             dma((K,)),
             dma((K, 2, 2, 3)),
@@ -362,13 +378,32 @@
             dma((NDP - 1,)),
             dma((NZ - 1,)),
             dma((NZ - 1,)),
-            dma((4,)),
+            dma((2,)),
             dma((4,)),
         ],
         compiler_params=pltpu.CompilerParams(
-            collective_id=0, has_side_effects=True, vmem_limit_bytes=48 * 1024 * 1024
+            collective_id=0, has_side_effects=True, vmem_limit_bytes=60 * 1024 * 1024
         ),
-    )(gate_partials, up_partials, gate_weight, up_weight, row_state, col_state)
+    )(gate_partials, up_partials, row_state, col_state)
+    return pl.pallas_call(
+        apply,
+        out_shape=(
+            jax.ShapeDtypeStruct((16, BLOCK), f32),
+            jax.ShapeDtypeStruct((16, BLOCK), f32),
+            jax.ShapeDtypeStruct((2, 16), f32),
+            jax.ShapeDtypeStruct((2, BLOCK), f32),
+        ),
+        in_specs=[pl.BlockSpec(memory_space=pl.ANY)] * 6,
+        out_specs=(pl.BlockSpec(memory_space=pl.ANY),) * 4,
+        scratch_shapes=[
+            pltpu.VMEM((2, 16, BLOCK), f32),
+            pltpu.VMEM((1, LANE), f32),
+            pltpu.VMEM((2, 16, BLOCK), f32),
+            dma((5,)),
+            dma((4,)),
+        ],
+        compiler_params=pltpu.CompilerParams(vmem_limit_bytes=60 * 1024 * 1024),
+    )(shape, sums, new_rows, new_cols, gate_weight, up_weight)
 
 
 def solution(mesh):

time: 72 us -> 61.2 us (0.85)
  local copies, waits for them, and re-layouts: 9.03 us -> 0 us
  Pallas kernels: 62 us -> 60.4 us
    unnamed x16 -> x0, local copies, waits for them, and re-layouts: 9.03 us -> none
    pallas_call x1 -> x2, Pallas kernels: 62 us -> 60.4 us  [the longest x1 58.5 us: on_device(): pl.pallas_call(kernel, out_shape=(jax.ShapeDtypeStruct((2, 16, BLOCK), f3...]
where the time goes in v2:
time: 61.2 us; the launch traced here: 61.1 us
  Pallas kernels  60.4 us (99%)
  between operations  0.64 us (1%)
    pallas_call x1, Pallas kernels, on_device(): pl.pallas_call(kernel, out_shape=(jax.ShapeDtypeStruct((2, 16, BLOCK), f3...  58.5 us
    pallas_call x1, Pallas kernels, on_device(): pl.pallas_call(apply, out_shape=(jax.ShapeDtypeStruct((16, BLOCK), f32),...  1.88 us

profile of v2, /device:TPU:1, one launch (start us, length us, event | category | flops | bytes accessed | tf_op | source)
XLA Modules:
  0.0 61.1 jit_solution(2337314078219878748)
XLA Ops:
  0.6 58.5 %shard_map.93 = (f32[2,16,2304]{2,1,0:T(8,128)}, f32[1,128]{1,0:T(1,128)}, f32[2,16]{1,0:T(2,128)}, f32[2,2304]{1,0:T(2,128)}) custom-call(bf16[1,16,73728]{2,1,0:T(8,128)(2,1)} %gate_hbm.1, bf16[1,16,73728]{2,1,0:T(8,128)(2,1)} %up_hbm.1, f32[2,16]{1,0:T(2,128)} %rows_hbm.1, f32[2,2304]{1,0:T(2,128)} %cols_hbm.1), custom_call_target="tpu_custom_call" | custom-call | tf_op jit(solution)/shard_map/pallas_call | solution.py:339
  59.2 1.9 %shard_map.94 = (f32[16,2304]{1,0:T(8,128)}, f32[16,2304]{1,0:T(8,128)}, f32[2,16]{1,0:T(2,128)}, f32[2,2304]{1,0:T(2,128)}) custom-call(f32[2,16,2304]{2,1,0:T(8,128)} %get-tuple-element.8.shape_hbm, f32[1,128]{1,0:T(1,128)} %get-tuple-element.9.sums_hbm, f32[2,16]{1,0:T(2,128)} %get-tuple-element.10.rows_hbm, f32[2,2304]{1,0:T(2,128)} %get-tuple-element.11.cols_hbm, ...), custom_call_target="tpu_custom_call" | custom-call | tf_op jit(solution)/shard_map/pallas_call | solution.py:388

commit v3 on v2

--- a/solution.py
+++ b/solution.py
@@ -16,9 +16,12 @@
 BLOCK = FF // NDP
 HALF = 8
 LANE = 128
-WIDE = 3 * LANE
-CHUNKS = tuple((m, j * 2 * WIDE, WIDE) for m in range(2) for j in range(BLOCK // (2 * WIDE)))
+TILES = ((3, 6), (6, 3))
+CHUNKS = tuple(
+    (m, 2 * LANE * sum(TILES[m][:j]), LANE * n) for m in range(2) for j, n in enumerate(TILES[m])
+)
 K = len(CHUNKS)
+SHORT = 0
 MESH = pl.DeviceIdType.MESH
 
 
@@ -82,14 +85,14 @@
             value = own_block(k, i, 1 - c)
             for h in range(2):
                 part = value[:, h * wide : (h + 1) * wide]
-                give[k, 0, h, rx, ry] = part[:HALF]
-                give[k, 1, h, ry, rx] = part[HALF:]
+                give[k][0, h, rx, ry] = part[:HALF]
+                give[k][1, h, ry, rx] = part[HALF:]
             return carry
 
         lax.fori_loop(0, NY * NX, one, 0, unroll=4)
 
     def exchange(k):
-        return send(give.at[k], work.at[k], core_send.at[k], core_recv.at[k], sibling)
+        return send(give[k], work[k], core_send.at[k], core_recv.at[k], sibling)
 
     def add_own(k):
         wide = CHUNKS[k][2]
@@ -99,8 +102,8 @@
             value = own_block(k, i, c)
             for h in range(2):
                 part = value[:, h * wide : (h + 1) * wide]
-                work[k, 0, h, rx, ry] = work[k, 0, h, rx, ry] + part[:HALF]
-                work[k, 1, h, ry, rx] = work[k, 1, h, ry, rx] + part[HALF:]
+                work[k][0, h, rx, ry] = work[k][0, h, rx, ry] + part[:HALF]
+                work[k][1, h, ry, rx] = work[k][1, h, ry, rx] + part[HALF:]
             return carry
 
         lax.fori_loop(0, NY * NX, one, 0, unroll=4)
@@ -113,40 +116,53 @@
         for p, h in pairs:
             step = (step_x, step_y)[p]
             copies[k, p, h, "far"] = send(
-                work.at[k, p, h, 2], far.at[k, p, h], s1_send.at[k, p, h, 0], s1_recv.at[k, p, h, 0], step[h])
+                work[k].at[p, h, 2], far[k].at[p, h], s1_send.at[k, p, h, 0], s1_recv.at[k, p, h, 0], step[h])
         for p, h in pairs:
             step = (step_x, step_y)[p]
             copies[k, p, h, "direct"] = send(
-                work.at[k, p, h, near[1 - h]], direct.at[k, p, h], s1_send.at[k, p, h, 1], s1_recv.at[k, p, h, 1],
+                work[k].at[p, h, near[1 - h]], direct[k].at[p, h], s1_send.at[k, p, h, 1], s1_recv.at[k, p, h, 1],
                 step[1 - h])
 
     def first_join(k):
         for p, h in pairs:
             step = (step_x, step_y)[p]
             copies[k, p, h, "far"].wait_recv()
-            work[k, p, h, near[h]] = work[k, p, h, near[h]] + far[k, p, h]
+            work[k][p, h, near[h]] = work[k][p, h, near[h]] + far[k][p, h]
             copies[k, p, h, "acc"] = send(
-                work.at[k, p, h, near[h]], acc.at[k, p, h], s1_send.at[k, p, h, 2], s1_recv.at[k, p, h, 2], step[h])
+                work[k].at[p, h, near[h]], acc[k].at[p, h], s1_send.at[k, p, h, 2], s1_recv.at[k, p, h, 2], step[h])
 
     def second_sends(k):
         for p, h in pairs:
             step = (step_y, step_x)[p]
             copies[k, p, h, "direct"].wait_recv()
             copies[k, p, h, "acc"].wait_recv()
-            work[k, p, h, 0] = work[k, p, h, 0] + direct[k, p, h] + acc[k, p, h]
+            work[k][p, h, 0] = work[k][p, h, 0] + direct[k][p, h] + acc[k][p, h]
+            if k >= K - SHORT:
+                opposite = (device(z, y + 2, x, c), device(z, y, x + 2, c))[p]
+                copies[k, p, h, "far2"] = send(
+                    work[k].at[p, h, 0, 2], far2[k].at[p, h], s2_send.at[k, p, h, 0], s2_recv.at[k, p, h, 0], opposite)
+                copies[k, p, h, "acc2"] = send(
+                    work[k].at[p, h, 0, near[h]], acc2[k].at[p, h], s2_send.at[k, p, h, 2], s2_recv.at[k, p, h, 2],
+                    step[h])
+                copies[k, p, h, "direct2"] = send(
+                    work[k].at[p, h, 0, near[1 - h]], direct2[k].at[p, h], s2_send.at[k, p, h, 1],
+                    s2_recv.at[k, p, h, 1], step[1 - h])
+                continue
             copies[k, p, h, "far2"] = send(
-                work.at[k, p, h, 0, 2], far2.at[k, p, h], s2_send.at[k, p, h, 0], s2_recv.at[k, p, h, 0], step[h])
+                work[k].at[p, h, 0, 2], far2[k].at[p, h], s2_send.at[k, p, h, 0], s2_recv.at[k, p, h, 0], step[h])
             copies[k, p, h, "direct2"] = send(
-                work.at[k, p, h, 0, near[1 - h]], direct2.at[k, p, h], s2_send.at[k, p, h, 1],
+                work[k].at[p, h, 0, near[1 - h]], direct2[k].at[p, h], s2_send.at[k, p, h, 1],
                 s2_recv.at[k, p, h, 1], step[1 - h])
 
     def second_join(k):
+        if k >= K - SHORT:
+            return
         for p, h in pairs:
             step = (step_y, step_x)[p]
             copies[k, p, h, "far2"].wait_recv()
-            work[k, p, h, 0, near[h]] = work[k, p, h, 0, near[h]] + far2[k, p, h]
+            work[k][p, h, 0, near[h]] = work[k][p, h, 0, near[h]] + far2[k][p, h]
             copies[k, p, h, "acc2"] = send(
-                work.at[k, p, h, 0, near[h]], acc2.at[k, p, h], s2_send.at[k, p, h, 2], s2_recv.at[k, p, h, 2],
+                work[k].at[p, h, 0, near[h]], acc2[k].at[p, h], s2_send.at[k, p, h, 2], s2_recv.at[k, p, h, 2],
                 step[h])
 
     lane_sums = [None, None]
@@ -162,13 +178,16 @@
         for p, h in pairs:
             copies[k, p, h, "direct2"].wait_recv()
             copies[k, p, h, "acc2"].wait_recv()
-            grad[m, p * HALF : (p + 1) * HALF, first + h * wide : first + (h + 1) * wide] = (
-                work[k, p, h, 0, 0] + direct2[k, p, h] + acc2[k, p, h])
+            total = work[k][p, h, 0, 0] + direct2[k][p, h] + acc2[k][p, h]
+            if k >= K - SHORT:
+                copies[k, p, h, "far2"].wait_recv()
+                total = total + far2[k][p, h]
+            grad[m, p * HALF : (p + 1) * HALF, first + h * wide : first + (h + 1) * wide] = total
         g = grad[m, :, first : first + 2 * wide]
         squares = g * g
-        col_all[k, z] = jnp.sum(squares, axis=0, keepdims=True)
+        col_all[k][z] = jnp.sum(squares, axis=0, keepdims=True)
         for i, peer in enumerate(column):
-            send(col_all.at[k, z], col_all.at[k, z], col_send.at[k, i], col_recv.at[k, i], peer)
+            send(col_all[k].at[z], col_all[k].at[z], col_send.at[k, i], col_recv.at[k, i], peer)
         part = lanes(squares)
         lane_sums[m] = part if lane_sums[m] is None else lane_sums[m] + part
 
@@ -176,7 +195,7 @@
         for i in range(NZ - 1):
             source = lax.rem(z + NZ - (4, 3, 5, 2, 6, 1, 7)[i], NZ)
             pltpu.make_async_remote_copy(
-                src_ref=col_all.at[k, source], dst_ref=col_all.at[k, source], send_sem=col_send.at[k, i],
+                src_ref=col_all[k].at[source], dst_ref=col_all[k].at[source], send_sem=col_send.at[k, i],
                 recv_sem=col_recv.at[k, i], device_id=sibling, device_id_type=MESH).wait_recv()
 
     for k in range(K):
@@ -220,9 +239,9 @@
     for k in range(K):
         m, first, wide = CHUNKS[k]
         wait_columns(k)
-        total = col_all[k, 0]
+        total = col_all[k][0]
         for j in range(1, NZ):
-            total = total + col_all[k, j]
+            total = total + col_all[k][j]
         span = slice(first, first + 2 * wide)
         fresh = DECAY * col_state[m : m + 1, span] + (1.0 - DECAY) * total / ROWS
         new_cols[m : m + 1, span] = fresh
@@ -296,37 +315,26 @@
 
 
 def apply(
-    shape_hbm, sums_hbm, rows_hbm, cols_hbm, gate_w_hbm, up_w_hbm,
+    shape, sums, rows, cols, gate_w, up_w,
     new_gate_hbm, new_up_hbm, new_rows_hbm, new_cols_hbm,
-    shape, sums, weight, in_sem, out_sem,
+    result, out_sem,
 ):
-    loads = [
-        pltpu.make_async_copy(src, dst, in_sem.at[i])
-        for i, (src, dst) in enumerate((
-            (sums_hbm, sums), (shape_hbm.at[0], shape.at[0]), (gate_w_hbm, weight.at[0]),
-            (shape_hbm.at[1], shape.at[1]), (up_w_hbm, weight.at[1])))
+    outs = [
+        pltpu.make_async_copy(rows, new_rows_hbm, out_sem.at[2]),
+        pltpu.make_async_copy(cols, new_cols_hbm, out_sem.at[3]),
     ]
-    outs = [
-        pltpu.make_async_copy(rows_hbm, new_rows_hbm, out_sem.at[2]),
-        pltpu.make_async_copy(cols_hbm, new_cols_hbm, out_sem.at[3]),
-    ]
-    for copy in loads + outs:
+    for copy in outs:
         copy.start()
-    loads[0].wait()
     lane = lax.broadcasted_iota(jnp.int32, (1, LANE), 1)
     total = sums[...]
-    scales = []
     for m in range(2):
         squares = jnp.sum(jnp.where(lane == m, total, 0.0), axis=1, keepdims=True)
         mean = jnp.sum(jnp.where(lane == 2 + m, total, 0.0), axis=1, keepdims=True) / ROWS
         root = jnp.sqrt(mean)
         rms = root * jnp.sqrt(squares / (ROWS * FF))
-        scales.append(STEP * root / jnp.maximum(1.0, rms))
-    for m in range(2):
-        loads[1 + 2 * m].wait()
-        loads[2 + 2 * m].wait()
-        weight[m] = weight[m] - shape[m] * scales[m]
-        out = pltpu.make_async_copy(weight.at[m], (new_gate_hbm, new_up_hbm)[m], out_sem.at[m])
+        scale = STEP * root / jnp.maximum(1.0, rms)
+        result[m] = (gate_w, up_w)[m][...] - shape[m] * scale
+        out = pltpu.make_async_copy(result.at[m], (new_gate_hbm, new_up_hbm)[m], out_sem.at[m])
         out.start()
         outs.append(out)
     for out in outs:
@@ -344,24 +352,24 @@
             jax.ShapeDtypeStruct((2, 16), f32),
             jax.ShapeDtypeStruct((2, BLOCK), f32),
         ),
-        in_specs=[pl.BlockSpec(memory_space=pl.ANY)] * 4,
+        in_specs=[pl.BlockSpec(memory_space=pltpu.HBM)] * 4,
         out_specs=(pl.BlockSpec(memory_space=pl.ANY),) * 4,
         scratch_shapes=[
             pltpu.VMEM((2, 16, FF), jnp.bfloat16),
-            pltpu.VMEM((K, 2, 2, 4, 4, HALF, WIDE), f32),
-            pltpu.VMEM((K, 2, 2, 4, 4, HALF, WIDE), f32),
-            pltpu.VMEM((K, 2, 2, 4, HALF, WIDE), f32),
-            pltpu.VMEM((K, 2, 2, 4, HALF, WIDE), f32),
-            pltpu.VMEM((K, 2, 2, 4, HALF, WIDE), f32),
-            pltpu.VMEM((K, 2, 2, HALF, WIDE), f32),
-            pltpu.VMEM((K, 2, 2, HALF, WIDE), f32),
-            pltpu.VMEM((K, 2, 2, HALF, WIDE), f32),
+            tuple(pltpu.VMEM((2, 2, 4, 4, HALF, wide), f32) for _, _, wide in CHUNKS),
+            tuple(pltpu.VMEM((2, 2, 4, 4, HALF, wide), f32) for _, _, wide in CHUNKS),
+            tuple(pltpu.VMEM((2, 2, 4, HALF, wide), f32) for _, _, wide in CHUNKS),
+            tuple(pltpu.VMEM((2, 2, 4, HALF, wide), f32) for _, _, wide in CHUNKS),
+            tuple(pltpu.VMEM((2, 2, 4, HALF, wide), f32) for _, _, wide in CHUNKS),
+            tuple(pltpu.VMEM((2, 2, HALF, wide), f32) for _, _, wide in CHUNKS),
+            tuple(pltpu.VMEM((2, 2, HALF, wide), f32) for _, _, wide in CHUNKS),
+            tuple(pltpu.VMEM((2, 2, HALF, wide), f32) for _, _, wide in CHUNKS),
             pltpu.VMEM((2, 16, BLOCK), f32),
             pltpu.VMEM((2, 16), f32),
             pltpu.VMEM((2, BLOCK), f32),
             pltpu.VMEM((2, 16), f32),
             pltpu.VMEM((2, BLOCK), f32),
-            pltpu.VMEM((K, NZ, 1, 2 * WIDE), f32),
+            tuple(pltpu.VMEM((NZ, 1, 2 * wide), f32) for _, _, wide in CHUNKS),
             pltpu.VMEM((NDP, 1, LANE), f32),
             pltpu.VMEM((NZ, 1, LANE), f32),
             pltpu.VMEM((1, LANE), f32),
@@ -382,7 +390,7 @@
             dma((4,)),
         ],
         compiler_params=pltpu.CompilerParams(
-            collective_id=0, has_side_effects=True, vmem_limit_bytes=60 * 1024 * 1024
+            collective_id=0, has_side_effects=True, vmem_limit_bytes=53 * 1024 * 1024
         ),
     )(gate_partials, up_partials, row_state, col_state)
     return pl.pallas_call(
@@ -393,16 +401,13 @@
             jax.ShapeDtypeStruct((2, 16), f32),
             jax.ShapeDtypeStruct((2, BLOCK), f32),
         ),
-        in_specs=[pl.BlockSpec(memory_space=pl.ANY)] * 6,
+        in_specs=[pl.BlockSpec(memory_space=pltpu.VMEM)] * 6,
         out_specs=(pl.BlockSpec(memory_space=pl.ANY),) * 4,
         scratch_shapes=[
             pltpu.VMEM((2, 16, BLOCK), f32),
-            pltpu.VMEM((1, LANE), f32),
-            pltpu.VMEM((2, 16, BLOCK), f32),
-            dma((5,)),
             dma((4,)),
         ],
-        compiler_params=pltpu.CompilerParams(vmem_limit_bytes=60 * 1024 * 1024),
+        compiler_params=pltpu.CompilerParams(vmem_limit_bytes=53 * 1024 * 1024),
     )(shape, sums, new_rows, new_cols, gate_weight, up_weight)
 
 

time: 61.2 us -> 60.1 us (0.982)
  Pallas kernels: 60.4 us -> 57.9 us
  local copies, waits for them, and re-layouts: 0 us -> 1.45 us
    pallas_call x1, Pallas kernels: 58.5 us -> 57 us  [on_device(): pl.pallas_call(kernel, out_shape=(jax.ShapeDtypeStruct((2, 16, BLOCK), f3...]
    unnamed x0 -> x8, local copies, waits for them, and re-layouts: none -> 1.45 us
    pallas_call x1, Pallas kernels: 1.88 us -> 0.86 us  [on_device(): pl.pallas_call(apply, out_shape=(jax.ShapeDtypeStruct((16, BLOCK), f32),...]
where the time goes in v3:
time: 60.1 us; the launch traced here: 60 us
  Pallas kernels  57.9 us (96%)
  local copies, waits for them, and re-layouts  1.45 us (2%)
  between operations  0.68 us (1%)
    pallas_call x1, Pallas kernels, on_device(): pl.pallas_call(kernel, out_shape=(jax.ShapeDtypeStruct((2, 16, BLOCK), f3...  57 us
    unnamed x8, local copies, waits for them, and re-layouts  1.45 us

profile of v3, /device:TPU:1, one launch (start us, length us, event | category | flops | bytes accessed | tf_op | source)
XLA Modules:
  0.0 60.0 jit_solution(9633064446129464500)
XLA Ops:
  0.6 0.0 copy-start.1
  0.6 0.0 copy-start
  0.7 0.0 copy-start.2
  0.7 0.8 %copy-done.2 = f32[2,2304]{1,0:T(2,128)S(1)} copy-done((f32[2,2304]{1,0:T(2,128)S(1)}, f32[2,2304]{1,0:T(2,128)}, u32[]{:S(2)}) %copy-start.2) | copy-done | bytes 18456
  1.4 0.0 copy-start.3
  1.4 0.7 %copy-done.3 = f32[2,16]{1,0:T(2,128)S(1)} copy-done((f32[2,16]{1,0:T(2,128)S(1)}, f32[2,16]{1,0:T(2,128)}, u32[]{:S(2)}) %copy-start.3) | copy-done | bytes 152
  2.1 57.0 %shard_map.93 = (f32[2,16,2304]{2,1,0:T(8,128)S(1)}, f32[1,128]{1,0:T(1,128)S(1)}, f32[2,16]{1,0:T(2,128)S(1)}, f32[2,2304]{1,0:T(2,128)S(1)}) custom-call(bf16[1,16,73728]{2,1,0:T(8,128)(2,1)} %gate_hbm.1, bf16[1,16,73728]{2,1,0:T(8,128)(2,1)} %up_hbm.1, f32[2,16]{1,0:T(2,128)S(1)} %copy-done.3, f32[2,2304]{1,0:T(2,128)S(1)} %copy-done.2), custom_call_target="tpu_custom_call" | custom-call | tf_op jit(solution)/shard_map/pallas_call | solution.py:347
  59.1 0.0 copy-done.1
  59.1 0.0 copy-done
  59.1 0.9 %shard_map.94 = (f32[16,2304]{1,0:T(8,128)}, f32[16,2304]{1,0:T(8,128)}, f32[2,16]{1,0:T(2,128)}, f32[2,2304]{1,0:T(2,128)}) custom-call(f32[2,16,2304]{2,1,0:T(8,128)S(1)} %get-tuple-element.8.shape, f32[1,128]{1,0:T(1,128)S(1)} %get-tuple-element.9.sums, f32[2,16]{1,0:T(2,128)S(1)} %get-tuple-element.10.rows, f32[2,2304]{1,0:T(2,128)S(1)} %get-tuple-element.11.cols, ...), custom_call_target="tpu_custom_call" | custom-call | tf_op jit(solution)/shard_map/pallas_call | solution.py:396
Async XLA Ops:
  0.6 58.5 %copy-start.1 = (f32[16,2304]{1,0:T(8,128)S(1)}, f32[16,2304]{1,0:T(8,128)}, u32[]{:S(2)}) copy-start(f32[16,2304]{1,0:T(8,128)} %up_w.1) | copy-start | bytes 442372
  0.6 58.5 %copy-start = (f32[16,2304]{1,0:T(8,128)S(1)}, f32[16,2304]{1,0:T(8,128)}, u32[]{:S(2)}) copy-start(f32[16,2304]{1,0:T(8,128)} %gate_w.1) | copy-start | bytes 442372
  0.7 0.8 %copy-start.2 = (f32[2,2304]{1,0:T(2,128)S(1)}, f32[2,2304]{1,0:T(2,128)}, u32[]{:S(2)}) copy-start(f32[2,2304]{1,0:T(2,128)} %cols_hbm.1) | copy-start | bytes 55300
  1.4 0.7 %copy-start.3 = (f32[2,16]{1,0:T(2,128)S(1)}, f32[2,16]{1,0:T(2,128)}, u32[]{:S(2)}) copy-start(f32[2,16]{1,0:T(2,128)} %rows_hbm.1) | copy-start | bytes 388

commit v4 on v3

--- a/solution.py
+++ b/solution.py
@@ -21,15 +21,14 @@
     (m, 2 * LANE * sum(TILES[m][:j]), LANE * n) for m in range(2) for j, n in enumerate(TILES[m])
 )
 K = len(CHUNKS)
-SHORT = 0
 MESH = pl.DeviceIdType.MESH
 
 
 def kernel(
-    gate_hbm, up_hbm, rows_hbm, cols_hbm,
+    gate_hbm, up_hbm, states_hbm,
     shape_hbm, sums_hbm, new_rows_hbm, new_cols_hbm,
     inb, give, work, far, acc, direct, far2, acc2, direct2, grad,
-    row_state, col_state, new_rows, new_cols, col_all, row_all, sum_all, sums,
+    states, new_rows, new_cols, col_all, row_all, sum_all, sums,
     in_sem, core_send, core_recv, s1_send, s1_recv, s2_send, s2_recv,
     col_send, col_recv, row_send, row_recv, sum_send, sum_recv, w_sem, out_sem,
 ):
@@ -58,8 +57,7 @@
     greeted = [*step_x, *step_y, sibling, *column]
     for peer in greeted:
         pl.semaphore_signal(barrier, 1, device_id=peer, device_id_type=MESH)
-    pltpu.make_async_copy(rows_hbm, row_state, w_sem.at[0]).start()
-    pltpu.make_async_copy(cols_hbm, col_state, w_sem.at[1]).start()
+    pltpu.make_async_copy(states_hbm, states, w_sem.at[0]).start()
 
     def own_block(k, i, core):
         m, first, wide = CHUNKS[k]
@@ -89,7 +87,7 @@
                 give[k][1, h, ry, rx] = part[HALF:]
             return carry
 
-        lax.fori_loop(0, NY * NX, one, 0, unroll=4)
+        lax.fori_loop(0, NY * NX, one, 0, unroll=16)
 
     def exchange(k):
         return send(give[k], work[k], core_send.at[k], core_recv.at[k], sibling)
@@ -106,7 +104,7 @@
                 work[k][1, h, ry, rx] = work[k][1, h, ry, rx] + part[HALF:]
             return carry
 
-        lax.fori_loop(0, NY * NX, one, 0, unroll=4)
+        lax.fori_loop(0, NY * NX, one, 0, unroll=16)
 
     near = (1, 3)
     pairs = [(p, h) for h in range(2) for p in range(2)]
@@ -137,17 +135,6 @@
             copies[k, p, h, "direct"].wait_recv()
             copies[k, p, h, "acc"].wait_recv()
             work[k][p, h, 0] = work[k][p, h, 0] + direct[k][p, h] + acc[k][p, h]
-            if k >= K - SHORT:
-                opposite = (device(z, y + 2, x, c), device(z, y, x + 2, c))[p]
-                copies[k, p, h, "far2"] = send(
-                    work[k].at[p, h, 0, 2], far2[k].at[p, h], s2_send.at[k, p, h, 0], s2_recv.at[k, p, h, 0], opposite)
-                copies[k, p, h, "acc2"] = send(
-                    work[k].at[p, h, 0, near[h]], acc2[k].at[p, h], s2_send.at[k, p, h, 2], s2_recv.at[k, p, h, 2],
-                    step[h])
-                copies[k, p, h, "direct2"] = send(
-                    work[k].at[p, h, 0, near[1 - h]], direct2[k].at[p, h], s2_send.at[k, p, h, 1],
-                    s2_recv.at[k, p, h, 1], step[1 - h])
-                continue
             copies[k, p, h, "far2"] = send(
                 work[k].at[p, h, 0, 2], far2[k].at[p, h], s2_send.at[k, p, h, 0], s2_recv.at[k, p, h, 0], step[h])
             copies[k, p, h, "direct2"] = send(
@@ -155,8 +142,6 @@
                 s2_recv.at[k, p, h, 1], step[1 - h])
 
     def second_join(k):
-        if k >= K - SHORT:
-            return
         for p, h in pairs:
             step = (step_y, step_x)[p]
             copies[k, p, h, "far2"].wait_recv()
@@ -179,9 +164,6 @@
             copies[k, p, h, "direct2"].wait_recv()
             copies[k, p, h, "acc2"].wait_recv()
             total = work[k][p, h, 0, 0] + direct2[k][p, h] + acc2[k][p, h]
-            if k >= K - SHORT:
-                copies[k, p, h, "far2"].wait_recv()
-                total = total + far2[k][p, h]
             grad[m, p * HALF : (p + 1) * HALF, first + h * wide : first + (h + 1) * wide] = total
         g = grad[m, :, first : first + 2 * wide]
         squares = g * g
@@ -228,10 +210,9 @@
     small_lane = lax.broadcasted_iota(jnp.int32, (16, 16), 1)
 
     row_sums = [jnp.sum(lane_sums[m], axis=1, keepdims=True) for m in range(2)]
-    for i, ref in enumerate((row_state, col_state)):
-        pltpu.make_async_copy(ref, ref, w_sem.at[i]).wait()
+    pltpu.make_async_copy(states, states, w_sem.at[0]).wait()
     old_rows = [
-        jnp.sum(jnp.where(small_row == small_lane, row_state[m : m + 1, :], 0.0), axis=1, keepdims=True)
+        jnp.sum(jnp.where(small_row == small_lane, states[m : m + 1, BLOCK:], 0.0), axis=1, keepdims=True)
         for m in range(2)
     ]
 
@@ -243,7 +224,7 @@
         for j in range(1, NZ):
             total = total + col_all[k][j]
         span = slice(first, first + 2 * wide)
-        fresh = DECAY * col_state[m : m + 1, span] + (1.0 - DECAY) * total / ROWS
+        fresh = DECAY * states[m : m + 1, span] + (1.0 - DECAY) * total / ROWS
         new_cols[m : m + 1, span] = fresh
         g = grad[m, :, span]
         part = lanes(g * g * (1.0 / fresh))
@@ -352,7 +333,7 @@
             jax.ShapeDtypeStruct((2, 16), f32),
             jax.ShapeDtypeStruct((2, BLOCK), f32),
         ),
-        in_specs=[pl.BlockSpec(memory_space=pltpu.HBM)] * 4,
+        in_specs=[pl.BlockSpec(memory_space=pltpu.HBM)] * 3,
         out_specs=(pl.BlockSpec(memory_space=pl.ANY),) * 4,
         scratch_shapes=[
             pltpu.VMEM((2, 16, FF), jnp.bfloat16),
@@ -365,8 +346,7 @@
             tuple(pltpu.VMEM((2, 2, HALF, wide), f32) for _, _, wide in CHUNKS),
             tuple(pltpu.VMEM((2, 2, HALF, wide), f32) for _, _, wide in CHUNKS),
             pltpu.VMEM((2, 16, BLOCK), f32),
-            pltpu.VMEM((2, 16), f32),
-            pltpu.VMEM((2, BLOCK), f32),
+            pltpu.VMEM((2, BLOCK + 16), f32),
             pltpu.VMEM((2, 16), f32),
             pltpu.VMEM((2, BLOCK), f32),
             tuple(pltpu.VMEM((NZ, 1, 2 * wide), f32) for _, _, wide in CHUNKS),
@@ -386,13 +366,13 @@
             dma((NDP - 1,)),
             dma((NZ - 1,)),
             dma((NZ - 1,)),
-            dma((2,)),
+            dma((1,)),
             dma((4,)),
         ],
         compiler_params=pltpu.CompilerParams(
             collective_id=0, has_side_effects=True, vmem_limit_bytes=53 * 1024 * 1024
         ),
-    )(gate_partials, up_partials, row_state, col_state)
+    )(gate_partials, up_partials, jnp.concatenate([col_state, row_state], axis=1))
     return pl.pallas_call(
         apply,
         out_shape=(

time: 60.1 us -> 59.4 us (0.988)
  local copies, waits for them, and re-layouts: 1.45 us -> 0.01 us
  other arithmetic: 0 us -> 0.75 us
    unnamed x8 -> x4, local copies, waits for them, and re-layouts: 1.45 us -> 0.01 us
    concatenate x0 -> x1, other arithmetic: none -> 0.75 us  [on_device(): jnp.concatenate([col_state, row_state], axis=1)]
where the time goes in v4:
time: 59.4 us; the launch traced here: 59.2 us
  Pallas kernels  57.8 us (97%)
  other arithmetic  0.75 us (1%)
  between operations  0.67 us (1%)
    pallas_call x1, Pallas kernels, on_device(): pl.pallas_call(kernel, out_shape=(jax.ShapeDtypeStruct((2, 16, BLOCK), f3...  56.9 us

profile of v4, /device:TPU:1, one launch (start us, length us, event | category | flops | bytes accessed | tf_op | source)
XLA Modules:
  0.0 59.2 jit_solution(9044667168885666986)
XLA Ops:
  0.6 0.7 %pad_maximum_fusion.states_hbm = f32[2,2320]{1,0:T(2,128)S(1)} fusion(f32[2,16]{1,0:T(2,128)} %param.10, f32[2,2304]{1,0:T(2,128)} %param.11), kind=kLoop, calls=%fused_computation | loop fusion | flops 4640 | bytes 37120 | tf_op jit(solution)/shard_map/concatenate | solution.py:375
  1.4 0.0 copy-start
  1.4 0.0 copy-start.1
  1.4 56.9 %shard_map.93 = (f32[2,16,2304]{2,1,0:T(8,128)S(1)}, f32[1,128]{1,0:T(1,128)S(1)}, f32[2,16]{1,0:T(2,128)S(1)}, f32[2,2304]{1,0:T(2,128)S(1)}) custom-call(bf16[1,16,73728]{2,1,0:T(8,128)(2,1)} %gate_hbm.1, bf16[1,16,73728]{2,1,0:T(8,128)(2,1)} %up_hbm.1, f32[2,2320]{1,0:T(2,128)S(1)} %pad_maximum_fusion.states_hbm), custom_call_target="tpu_custom_call" | custom-call | tf_op jit(solution)/shard_map/pallas_call | solution.py:328
  58.3 0.0 copy-done
  58.3 0.0 copy-done.1
  58.4 0.9 %shard_map.94 = (f32[16,2304]{1,0:T(8,128)}, f32[16,2304]{1,0:T(8,128)}, f32[2,16]{1,0:T(2,128)}, f32[2,2304]{1,0:T(2,128)}) custom-call(f32[2,16,2304]{2,1,0:T(8,128)S(1)} %get-tuple-element.8.shape, f32[1,128]{1,0:T(1,128)S(1)} %get-tuple-element.9.sums, f32[2,16]{1,0:T(2,128)S(1)} %get-tuple-element.10.rows, f32[2,2304]{1,0:T(2,128)S(1)} %get-tuple-element.11.cols, ...), custom_call_target="tpu_custom_call" | custom-call | tf_op jit(solution)/shard_map/pallas_call | solution.py:376
Async XLA Ops:
  1.4 56.9 %copy-start = (f32[16,2304]{1,0:T(8,128)S(1)}, f32[16,2304]{1,0:T(8,128)}, u32[]{:S(2)}) copy-start(f32[16,2304]{1,0:T(8,128)} %gate_w.1) | copy-start | bytes 442372
  1.4 56.9 %copy-start.1 = (f32[16,2304]{1,0:T(8,128)S(1)}, f32[16,2304]{1,0:T(8,128)}, u32[]{:S(2)}) copy-start(f32[16,2304]{1,0:T(8,128)} %up_w.1) | copy-start | bytes 442372

commit v5 on v4

--- a/solution.py
+++ b/solution.py
@@ -92,19 +92,18 @@
     def exchange(k):
         return send(give[k], work[k], core_send.at[k], core_recv.at[k], sibling)
 
-    def add_own(k):
+    every = [(ry, rx) for ry in range(NY) for rx in range(NX)]
+    far_first = [q for q in every if 2 in q]
+    others = [q for q in every if 2 not in q]
+
+    def add_own(k, blocks):
         wide = CHUNKS[k][2]
-
-        def one(i, carry):
-            ry, rx = i // NX, i % NX
-            value = own_block(k, i, c)
+        for ry, rx in blocks:
+            value = own_block(k, ry * NX + rx, c)
             for h in range(2):
                 part = value[:, h * wide : (h + 1) * wide]
                 work[k][0, h, rx, ry] = work[k][0, h, rx, ry] + part[:HALF]
                 work[k][1, h, ry, rx] = work[k][1, h, ry, rx] + part[HALF:]
-            return carry
-
-        lax.fori_loop(0, NY * NX, one, 0, unroll=16)
 
     near = (1, 3)
     pairs = [(p, h) for h in range(2) for p in range(2)]
@@ -115,6 +114,7 @@
             step = (step_x, step_y)[p]
             copies[k, p, h, "far"] = send(
                 work[k].at[p, h, 2], far[k].at[p, h], s1_send.at[k, p, h, 0], s1_recv.at[k, p, h, 0], step[h])
+        add_own(k, others)
         for p, h in pairs:
             step = (step_x, step_y)[p]
             copies[k, p, h, "direct"] = send(
@@ -189,10 +189,10 @@
         copies[k, "core"] = exchange(k)
         if k > 0:
             copies[k - 1, "core"].wait_recv()
-            add_own(k - 1)
+            add_own(k - 1, far_first)
             first_sends(k - 1)
     copies[K - 1, "core"].wait_recv()
-    add_own(K - 1)
+    add_own(K - 1, far_first)
     first_sends(K - 1)
     for k in range(K):
         first_join(k)

time: 59.4 us -> 59.3 us (level)
  no operation moved by 1% of the time
where the time goes in v5:
time: 59.3 us; the launch traced here: 59.2 us
  Pallas kernels  57.7 us (97%)
  other arithmetic  0.75 us (1%)
  between operations  0.67 us (1%)
    pallas_call x1, Pallas kernels, on_device(): pl.pallas_call(kernel, out_shape=(jax.ShapeDtypeStruct((2, 16, BLOCK), f3...  56.9 us

profile of v5, /device:TPU:1, one launch (start us, length us, event | category | flops | bytes accessed | tf_op | source)
XLA Modules:
  0.0 59.2 jit_solution(6876517384751780605)
XLA Ops:
  0.6 0.7 %pad_maximum_fusion.states_hbm = f32[2,2320]{1,0:T(2,128)S(1)} fusion(f32[2,16]{1,0:T(2,128)} %param.10, f32[2,2304]{1,0:T(2,128)} %param.11), kind=kLoop, calls=%fused_computation | loop fusion | flops 4640 | bytes 37120 | tf_op jit(solution)/shard_map/concatenate | solution.py:375
  1.4 0.0 copy-start
  1.4 0.0 copy-start.1
  1.4 56.9 %shard_map.93 = (f32[2,16,2304]{2,1,0:T(8,128)S(1)}, f32[1,128]{1,0:T(1,128)S(1)}, f32[2,16]{1,0:T(2,128)S(1)}, f32[2,2304]{1,0:T(2,128)S(1)}) custom-call(bf16[1,16,73728]{2,1,0:T(8,128)(2,1)} %gate_hbm.1, bf16[1,16,73728]{2,1,0:T(8,128)(2,1)} %up_hbm.1, f32[2,2320]{1,0:T(2,128)S(1)} %pad_maximum_fusion.states_hbm), custom_call_target="tpu_custom_call" | custom-call | tf_op jit(solution)/shard_map/pallas_call | solution.py:328
  58.3 0.0 copy-done
  58.3 0.0 copy-done.1
  58.3 0.9 %shard_map.94 = (f32[16,2304]{1,0:T(8,128)}, f32[16,2304]{1,0:T(8,128)}, f32[2,16]{1,0:T(2,128)}, f32[2,2304]{1,0:T(2,128)}) custom-call(f32[2,16,2304]{2,1,0:T(8,128)S(1)} %get-tuple-element.8.shape, f32[1,128]{1,0:T(1,128)S(1)} %get-tuple-element.9.sums, f32[2,16]{1,0:T(2,128)S(1)} %get-tuple-element.10.rows, f32[2,2304]{1,0:T(2,128)S(1)} %get-tuple-element.11.cols, ...), custom_call_target="tpu_custom_call" | custom-call | tf_op jit(solution)/shard_map/pallas_call | solution.py:376
Async XLA Ops:
  1.4 56.9 %copy-start = (f32[16,2304]{1,0:T(8,128)S(1)}, f32[16,2304]{1,0:T(8,128)}, u32[]{:S(2)}) copy-start(f32[16,2304]{1,0:T(8,128)} %gate_w.1) | copy-start | bytes 442372
  1.4 56.9 %copy-start.1 = (f32[16,2304]{1,0:T(8,128)S(1)}, f32[16,2304]{1,0:T(8,128)}, u32[]{:S(2)}) copy-start(f32[16,2304]{1,0:T(8,128)} %up_w.1) | copy-start | bytes 442372
